TPU v7x, 32 devices: a whole 2x2x4 slice. The times are simulated.
32 devices in a mesh: pair: 8 (over z, x), virt: 4 (over y, core).
Axes of the slice: x: 2, y: 2, z: 4, core: 2. Of those that a mesh axis runs over, the one named last changes fastest.
Arguments:
- t_amps: bfloat16 [4096, 1024], P('pair', 'virt'), may hold values from -6 to 6
- v_ints: bfloat16 [4096, 1024], P('virt', 'pair'), may hold values from -0.1875 to 0.1875
- t_mask: int32 [32, 8], P('pair', 'virt'), may hold values 0 or 1
- v_mask: int32 [32, 8], P('virt'), may hold values from 0 to 1, as said below
Outputs:
- ladder: bfloat16 [4096, 4096], P('pair', 'virt')
Inputs may be any that keep to these rules, and one draw needn't show every extreme that they name: `v_mask`: in each column and each aligned block of 8 rows (one device's ab tiles) between 1 and 4 entries are 1; in every column some block has exactly 4.
All inputs are finite; a program needn't handle non-finite values. No bound on the sum of `t_mask` on one device may be relied on, other than what follows from the above.
Results may differ from a plain program's by a relative error of at most 0.001.
Values may be sent and summed in bfloat16 or wider, within the bound.
A program may use at most 64 MiB of HBM per device.

v0:
```python
import jax
import jax.numpy as jnp
from jax import lax
from jax.sharding import PartitionSpec as P

TILE = 128
ABT_DEV = 8


def local(t_amps, v_ints, t_mask, v_mask):
    pair_tiles, cd_local = t_mask.shape
    rows = t_amps.shape[0]
    shaped = t_amps.reshape(pair_tiles, TILE, cd_local, TILE)
    masked_t = (shaped * t_mask.astype(jnp.bfloat16)[:, None, :, None]).reshape(
        rows, cd_local * TILE
    )
    t_full = lax.all_gather(masked_t, "virt", axis=1, tiled=True)
    ab_rows = v_ints.shape[0]
    my_index = lax.axis_index("pair")
    own_flags = lax.dynamic_slice_in_dim(v_mask, my_index, 1, 1)[:, 0]
    v_tiles = v_ints.reshape(ABT_DEV, TILE, TILE)
    v_masked = v_tiles * own_flags.astype(jnp.bfloat16)[:, None, None]
    total = lax.dot_general(
        t_full,
        lax.all_gather(v_masked.reshape(ab_rows, TILE), "pair", axis=1, tiled=True),
        (((1,), (1,)), ((), ())),
        preferred_element_type=jnp.float32,
    )
    return total.astype(jnp.bfloat16)


def solution(mesh):
    return jax.shard_map(
        local,
        mesh=mesh,
        in_specs=(P("pair", "virt"), P("virt", "pair"), P("pair", "virt"), P("virt", None)),
        out_specs=P("pair", "virt"),
        check_vma=False,
    )
```

profile of v0, /device:TPU:0, one launch (start us, length us, event | category | flops | bytes accessed | tf_op | source)
XLA Modules:
  0.0 93.2 jit_solution(6612220598665781263)
XLA Ops:
  6.5 0.0 all-gather.3.cloned.1.call-start
  6.5 0.7 convert_element_type.16
  7.2 0.1 copy.5
  7.3 0.2 mul.24
  7.5 1.7 %bitcast_multiply_fusion = bf16[512,256]{1,0:T(8,128)(2,1)} fusion(bf16[512,256]{1,0:T(8,128)(2,1)} %param.4, bf16[64,8,2,128]{3,2,1,0:T(2,128)(2,1)S(1)} %bitcast.8), kind=kLoop, calls=%fused_computation.1 | loop fusion | flops 131072 | bytes 786432 | tf_op jit(solution)/shard_map/mul | solution.py:14
  9.2 0.0 all-gather.3.cloned.1.call-update
  9.3 0.0 all-gather.5.cloned.1.call-start
  9.3 0.9 fusion
  10.2 0.1 broadcast_bitcast_fusion
  10.3 1.8 %broadcast_multiply_fusion = bf16[1024,128]{1,0:T(8,128)(2,1)} fusion(bf16[1024,128]{1,0:T(8,128)(2,1)} %param.5, bf16[1024]{0:T(1024)(128)(2,1)S(1)} %broadcast_bitcast_fusion), kind=kLoop, calls=%fused_computation.2 | loop fusion | flops 131072 | bytes 526336 | tf_op jit(solution)/shard_map/mul | solution.py:22
  12.1 0.0 all-gather.5.cloned.1.call-update
  12.1 16.9 %all-gather.3.cloned.1.call-done = bf16[512,1024]{1,0:T(8,128)(2,1)} async-done(((bf16[512,256]{1,0:T(8,128)(2,1)}), bf16[512,1024]{1,0:T(8,128)(2,1)}) %all-gather.3.cloned.1.call-update) | async-done | bytes 1048592 | tf_op jit(solution)/shard_map/all_gather | solution.py:17
  29.0 53.1 %all-gather.5.cloned.1.call-done = bf16[1024,1024]{1,0:T(8,128)(2,1)} async-done(((bf16[1024,128]{1,0:T(8,128)(2,1)}), bf16[1024,1024]{1,0:T(8,128)(2,1)}) %all-gather.5.cloned.1.call-update) | async-done | bytes 2097168 | tf_op jit(solution)/shard_map/all_gather | solution.py:25
  82.2 4.2 %convolution_convert_fusion = bf16[512,1024]{1,0:T(8,128)(2,1)} fusion(bf16[512,1024]{1,0:T(8,128)(2,1)} %all-gather.3.cloned.1.call-done, bf16[1024,1024]{1,0:T(8,128)(2,1)} %all-gather.5.cloned.1.call-done), kind=kOutput, calls=%fused_computation | convolution fusion | flops 1074266112 | bytes 4194304 | tf_op jit(solution)/shard_map/dot_general | solution.py:23
Async XLA Ops:
  6.5 22.5 %all-gather.3.cloned.1.call-start = ((), (), s32[]{:S(2)}) async-start(), calls=%async_computation | async-start | bytes 1310720 | tf_op jit(solution)/shard_map/all_gather | solution.py:17
  9.3 72.9 %all-gather.5.cloned.1.call-start = ((), (), s32[]{:S(2)}) async-start(), calls=%async_computation.1 | async-start | bytes 2359296 | tf_op jit(solution)/shard_map/all_gather | solution.py:25
Sparse Core Ops, SparseCore 0:
  9.4 19.5 all-gather.2
  31.1 51.0 all-gather.4
where the time goes:
time: 93.4 us; the launch traced here: 93.2 us
  waiting for transfers between devices  70.1 us (75%)
  between operations  13.4 us (14%)
  other arithmetic  5.1 us (5%)
  matrix products  4.18 us (4%)
    all_gather x1, waiting for transfers between devices, local(): lax.all_gather(v_masked.reshape(ab_rows, TILE), 'pair', axis=1, tiled=True)  53.1 us
    all_gather x1, waiting for transfers between devices, local(): t_full = lax.all_gather(masked_t, 'virt', axis=1, tiled=True)  16.9 us
    dot_general x1, matrix products, local(): lax.dot_general(t_full, lax.all_gather(v_masked.reshape(ab_rows, TILE), '...  4.18 us
  transfers between devices with their start and end apart: 2, of which 2 were waited for; matrix products, arithmetic and copies ran while one was open for 3% of the time, Pallas kernels for 0%

commit v1 on v0

v1 whole, which is shorter than its diff:
```python
import functools

import jax
import jax.numpy as jnp
from jax import lax
from jax.experimental import pallas as pl
from jax.experimental.pallas import tpu as pltpu
from jax.sharding import PartitionSpec as P

TILE = 128
VCAP = 4
NT = 256
MESH = pl.DeviceIdType.MESH


def nth_nearest(s, z, Z):
    low = jnp.minimum(z, Z - 1 - z)
    near = z - (s + 1) // 2 if s % 2 else z + s // 2
    far = jnp.where(z < Z - 1 - z, s, Z - 1 - s)
    return jnp.where(s <= 2 * low, near, far)


def kernel(
    Z, H, tm_ref, vm_ref, t_hbm, v_hbm, out_ref,
    t_in, v_in, tf, vc, stage, vd, acc,
    in_sem, v_recv, v_send, t_recv, t_far, t_near,
):
    ab_tiles = vm_ref.shape[0]
    me = lax.axis_index("pair")
    my_q = lax.axis_index("virt")
    z, x = me // 2, me % 2
    h, c = my_q // 2, my_q % 2
    up, down, side = me + 2, me - 2, 2 * z + (1 - x)
    sibling = 2 * h + (1 - c)

    load_v = pltpu.make_async_copy(v_hbm, v_in, in_sem.at[0])
    load_t = pltpu.make_async_copy(t_hbm, t_in, in_sem.at[1])
    load_v.start()
    load_t.start()

    barrier = pltpu.get_barrier_semaphore()

    def greet(pair, virt):
        pl.semaphore_signal(barrier, inc=1, device_id=(pair, virt), device_id_type=MESH)

    @pl.when(z > 0)
    def _():
        greet(down, my_q)

    @pl.when(z < Z - 1)
    def _():
        greet(up, my_q)

    greet(side, my_q)
    greet(me, sibling)
    for i in range(1, H):
        greet(me, 2 * lax.rem(h + i, H) + c)

    load_v.wait()
    seen = jnp.int32(0)
    picks = [jnp.int32(0)] * VCAP
    for i in range(ab_tiles):
        flag = vm_ref[i, me]
        for j in range(VCAP):
            picks[j] = jnp.where((flag != 0) & (seen == j), i, picks[j])
        seen = seen + flag
    for j in range(VCAP):
        vc[me, j] = v_in[picks[j]]

    pl.semaphore_wait(
        barrier,
        1 + H + jnp.where(z > 0, 1, 0) + jnp.where(z < Z - 1, 1, 0),
    )

    def v_copy(block, way, to):
        return pltpu.make_async_remote_copy(
            src_ref=vc.at[block],
            dst_ref=vc.at[block],
            send_sem=v_send.at[way, block],
            recv_sem=v_recv.at[block],
            device_id=(to, my_q),
            device_id_type=MESH,
        )

    def t_copy(block, sem, to):
        return pltpu.make_async_remote_copy(
            src_ref=tf.at[block],
            dst_ref=tf.at[block],
            send_sem=sem,
            recv_sem=t_recv.at[block],
            device_id=(me, to),
            device_id_type=MESH,
        )

    def pass_on(a):
        block = 2 * a + x

        @pl.when((a <= z) & (z < Z - 1))
        def _():
            v_copy(block, 0, up).start()

        @pl.when((a >= z) & (z > 0))
        def _():
            v_copy(block, 1, down).start()

        v_copy(block, 2, side).start()

    pass_on(z)

    load_t.wait()
    cd = tm_ref.shape[0]
    for i in range(tm_ref.shape[1]):
        for j in range(cd):
            rows, cols = pl.ds(i * TILE, TILE), pl.ds(j * TILE, TILE)
            flag = jnp.full((TILE, TILE), tm_ref[j, i].astype(jnp.float32))
            tf[my_q, rows, cols] = t_in[rows, cols] * flag.astype(jnp.bfloat16)
    for i in range(1, H):
        t_copy(my_q, t_far.at[i], 2 * lax.rem(h + i, H) + c).start()
    t_copy(my_q, t_near.at[my_q], sibling).start()

    stage[VCAP] = jnp.zeros((TILE, TILE), jnp.bfloat16)

    def expand(a):
        for j in range(2):
            k = 2 * a + j
            for i in range(VCAP):
                stage[i] = vc[k, i]
            rank = jnp.int32(0)
            for i in range(ab_tiles):
                flag = vm_ref[i, k]
                where = jnp.where(flag != 0, rank, VCAP)
                rank = rank + flag
                vd[pl.ds(i * TILE, TILE), pl.ds(j * TILE, TILE)] = stage[where]

    def multiply(a, s):
        expand(a)
        left = tf.at[a]

        @pl.loop(0, ab_tiles * TILE // NT)
        def _(n):
            cols = pl.ds(pl.multiple_of(n * NT, NT), NT)
            part = lax.dot_general(
                left[...], vd[cols, :], (((1,), (1,)), ((), ())),
                preferred_element_type=jnp.float32,
            )
            if s > 0:
                part = part + acc[:, cols]
            if s < Z - 1:
                acc[:, cols] = part
            else:
                out_ref[:, cols] = part.astype(out_ref.dtype)

    def take(s):
        a = nth_nearest(s, z, Z)
        v_copy(2 * a + x, 2, side).wait_recv()
        pass_on(a)

    def finish(s):
        a = nth_nearest(s, z, Z)
        v_copy(2 * a + (1 - x), 2, side).wait_recv()
        multiply(a, s)

    first = min(2, Z - 1)
    for s in range(1, first + 1):
        take(s)
    for i in range(1, H):
        block = 2 * lax.rem(h + H - i, H) + c
        t_copy(block, t_far.at[i], sibling).wait_recv()
        t_copy(block, t_near.at[block], sibling).start()
    for i in range(H):
        block = 2 * i + (1 - c)
        t_copy(block, t_near.at[block], sibling).wait_recv()
    for s in range(Z):
        if s > first:
            take(s)
        if s >= first:
            finish(s - first)
    for s in range(Z - first, Z):
        finish(s)

    for s in range(Z):
        a = nth_nearest(s, z, Z)
        block = 2 * a + x

        @pl.when((a <= z) & (z < Z - 1))
        def _():
            v_copy(block, 0, up).wait_send()

        @pl.when((a >= z) & (z > 0))
        def _():
            v_copy(block, 1, down).wait_send()

        v_copy(block, 2, side).wait_send()
    for i in range(1, H):
        t_copy(my_q, t_far.at[i], sibling).wait_send()
    for i in range(H):
        block = 2 * i + c
        t_copy(block, t_near.at[block], sibling).wait_send()


def local(n_pair, n_virt, t_amps, v_ints, t_mask, v_mask):
    rows, t_cols = t_amps.shape
    ab_rows, _ = v_ints.shape
    ab_tiles = ab_rows // TILE
    dma = pltpu.SemaphoreType.DMA
    bf16 = jnp.bfloat16
    return pl.pallas_call(
        functools.partial(kernel, n_pair // 2, n_virt // 2),
        out_shape=jax.ShapeDtypeStruct((rows, ab_rows), bf16),
        in_specs=[pl.BlockSpec(memory_space=pltpu.SMEM)] * 2
        + [pl.BlockSpec(memory_space=pl.ANY)] * 2,
        out_specs=pl.BlockSpec(memory_space=pltpu.VMEM),
        scratch_shapes=[
            pltpu.VMEM((rows, t_cols), bf16),
            pltpu.VMEM((ab_tiles, TILE, TILE), bf16),
            pltpu.VMEM((n_virt, rows, t_cols), bf16),
            pltpu.VMEM((n_pair, VCAP, TILE, TILE), bf16),
            pltpu.VMEM((VCAP + 1, TILE, TILE), bf16),
            pltpu.VMEM((ab_rows, 2 * TILE), bf16),
            pltpu.VMEM((rows, ab_rows), jnp.float32),
            dma((2,)),
            dma((n_pair,)),
            dma((3, n_pair)),
            dma((n_virt,)),
            dma((n_virt,)),
            dma((n_virt,)),
        ],
        compiler_params=pltpu.CompilerParams(
            collective_id=0, has_side_effects=True, vmem_limit_bytes=40 * 2**20
        ),
    )(t_mask.T, v_mask, t_amps, v_ints.reshape(ab_tiles, TILE, TILE))


def solution(mesh):
    return jax.shard_map(
        functools.partial(local, mesh.shape["pair"], mesh.shape["virt"]),
        mesh=mesh,
        in_specs=(P("pair", "virt"), P("virt", "pair"), P("pair", "virt"), P("virt", None)),
        out_specs=P("pair", "virt"),
        check_vma=False,
    )
```

time: 93.4 us -> 29.9 us (0.32)
  waiting for transfers between devices: 70.1 us -> 0 us
  Pallas kernels: 0 us -> 25.5 us
  between operations: 13.4 us -> 0.01 us
  other arithmetic: 5.1 us -> 0 us
  matrix products: 4.18 us -> 0 us
  local copies, waits for them, and re-layouts: 0.39 us -> 4.24 us
    all_gather x2 -> x0, waiting for transfers between devices: 70 us -> none  [the longest x1 53.1 us: local(): lax.all_gather(v_masked.reshape(ab_rows, TILE), 'pair', axis=1, tiled=True)]
    pallas_call x0 -> x1, Pallas kernels: none -> 25.5 us  [local(): pl.pallas_call(functools.partial(kernel, n_pair // 2, n_virt // 2), out_s...]
    unnamed x0 -> x9, local copies, waits for them, and re-layouts: none -> 4.24 us
    dot_general x1 -> x0, matrix products: 4.18 us -> none  [local(): lax.dot_general(t_full, lax.all_gather(v_masked.reshape(ab_rows, TILE), '...]
    mul x2 -> x0, other arithmetic: 3.55 us -> none  [the longest x1 1.85 us: local(): v_masked = v_tiles * own_flags.astype(jnp.bfloat16)[:, None, None]]
    convert_element_type x2 -> x0, other arithmetic: 1.56 us -> none  [the longest x1 0.87 us: local(): v_masked = v_tiles * own_flags.astype(jnp.bfloat16)[:, None, None]]
  transfers between devices with their start and end apart: 2 -> 0, of which waited for: 2 -> 0; matrix products, arithmetic and copies ran while one was open for 3% -> 0% of each run, Pallas kernels for 0% -> 0%
where the time goes in v1:
time: 29.9 us; the launch traced here: 29.7 us
  Pallas kernels  25.5 us (85%)
  local copies, waits for them, and re-layouts  4.24 us (14%)
    pallas_call x1, Pallas kernels, local(): pl.pallas_call(functools.partial(kernel, n_pair // 2, n_virt // 2), out_s...  25.5 us
    unnamed x9, local copies, waits for them, and re-layouts  4.24 us

profile of v1, /device:TPU:0, one launch (start us, length us, event | category | flops | bytes accessed | tf_op | source)
XLA Modules:
  0.0 29.7 jit_solution(17596847570559040972)
XLA Ops:
  0.0 0.0 copy-start.3
  0.0 0.7 %copy-done.3 = s32[4,2]{0,1:T(2,128)S(1)} copy-done((s32[4,2]{0,1:T(2,128)S(1)}, s32[4,2]{0,1:T(2,128)}, u32[]{:S(2)}) %copy-start.3) | copy-done | bytes 56
  0.7 0.0 copy-start
  0.7 0.9 %copy-done = bf16[512,256]{1,0:T(8,128)(2,1)S(1)} copy-done((bf16[512,256]{1,0:T(8,128)(2,1)S(1)}, bf16[512,256]{1,0:T(8,128)(2,1)}, u32[]{:S(2)}) %copy-start) | copy-done | bytes 262168
  1.6 0.0 copy-start.1
  1.6 0.9 %copy-done.1 = bf16[1024,128]{1,0:T(8,128)(2,1)S(1)} copy-done((bf16[1024,128]{1,0:T(8,128)(2,1)S(1)}, bf16[1024,128]{1,0:T(8,128)(2,1)}, u32[]{:S(2)}) %copy-start.1) | copy-done | bytes 262168
  2.6 0.0 copy-start.2
  2.6 0.7 %copy-done.2 = s32[8,8]{1,0:T(8,128)S(1)} copy-done((s32[8,8]{1,0:T(8,128)S(1)}, s32[8,8]{1,0:T(8,128)}, u32[]{:S(2)}) %copy-start.2) | copy-done | bytes 280
  3.3 25.5 %shard_map.46 = bf16[512,1024]{1,0:T(8,128)(2,1)S(1)} custom-call(s32[2,4]{1,0:T(2,128)S(1)} %bitcast.3, s32[8,8]{1,0:T(8,128)S(1)} %copy-done.2, bf16[512,256]{1,0:T(8,128)(2,1)S(1)} %copy-done, bf16[8,128,128]{2,1,0:T(8,128)(2,1)S(1)} %bitcast.2), custom_call_target="tpu_custom_call" | custom-call | tf_op jit(solution)/shard_map/pallas_call | solution.py:207
  28.8 1.0 %copy.6 = bf16[512,1024]{1,0:T(8,128)(2,1)} copy(bf16[512,1024]{1,0:T(8,128)(2,1)S(1)} %shard_map.46) | data formatting | bytes 2097152
Async XLA Ops:
  0.0 0.7 %copy-start.3 = (s32[4,2]{0,1:T(2,128)S(1)}, s32[4,2]{0,1:T(2,128)}, u32[]{:S(2)}) copy-start(s32[4,2]{0,1:T(2,128)} %param.6) | copy-start | bytes 100
  0.7 0.9 %copy-start = (bf16[512,256]{1,0:T(8,128)(2,1)S(1)}, bf16[512,256]{1,0:T(8,128)(2,1)}, u32[]{:S(2)}) copy-start(bf16[512,256]{1,0:T(8,128)(2,1)} %t_hbm.1) | copy-start | bytes 786436
  1.6 0.9 %copy-start.1 = (bf16[1024,128]{1,0:T(8,128)(2,1)S(1)}, bf16[1024,128]{1,0:T(8,128)(2,1)}, u32[]{:S(2)}) copy-start(bf16[1024,128]{1,0:T(8,128)(2,1)} %param.5) | copy-start | bytes 786436
  2.6 0.7 %copy-start.2 = (s32[8,8]{1,0:T(8,128)S(1)}, s32[8,8]{1,0:T(8,128)}, u32[]{:S(2)}) copy-start(s32[8,8]{1,0:T(8,128)} %vm_ref.1) | copy-start | bytes 772

commit v2 on v1

--- a/solution.py
+++ b/solution.py
@@ -9,6 +9,8 @@
 
 TILE = 128
 VCAP = 4
+CHUNKS = 2
+WINDOW = 3
 NT = 256
 MESH = pl.DeviceIdType.MESH
 
@@ -21,8 +23,8 @@
 
 
 def kernel(
-    Z, H, tm_ref, vm_ref, t_hbm, v_hbm, out_ref,
-    t_in, v_in, tf, vc, stage, vd, acc,
+    Z, H, tm_hbm, vm_hbm, t_hbm, v_hbm, out_ref,
+    tm_ref, vm_ref, t_in, v_in, tf, vc, stage, vd, acc,
     in_sem, v_recv, v_send, t_recv, t_far, t_near,
 ):
     ab_tiles = vm_ref.shape[0]
@@ -35,7 +37,11 @@
 
     load_v = pltpu.make_async_copy(v_hbm, v_in, in_sem.at[0])
     load_t = pltpu.make_async_copy(t_hbm, t_in, in_sem.at[1])
+    load_vm = pltpu.make_async_copy(vm_hbm, vm_ref, in_sem.at[2])
+    load_tm = pltpu.make_async_copy(tm_hbm, tm_ref, in_sem.at[3])
+    load_vm.start()
     load_v.start()
+    load_tm.start()
     load_t.start()
 
     barrier = pltpu.get_barrier_semaphore()
@@ -56,7 +62,7 @@
     for i in range(1, H):
         greet(me, 2 * lax.rem(h + i, H) + c)
 
-    load_v.wait()
+    load_vm.wait()
     seen = jnp.int32(0)
     picks = [jnp.int32(0)] * VCAP
     for i in range(ab_tiles):
@@ -64,6 +70,7 @@
         for j in range(VCAP):
             picks[j] = jnp.where((flag != 0) & (seen == j), i, picks[j])
         seen = seen + flag
+    load_v.wait()
     for j in range(VCAP):
         vc[me, j] = v_in[picks[j]]
 
@@ -72,12 +79,13 @@
         1 + H + jnp.where(z > 0, 1, 0) + jnp.where(z < Z - 1, 1, 0),
     )
 
-    def v_copy(block, way, to):
+    def v_copy(block, u, way, to):
+        part = pl.ds(u * (VCAP // CHUNKS), VCAP // CHUNKS)
         return pltpu.make_async_remote_copy(
-            src_ref=vc.at[block],
-            dst_ref=vc.at[block],
-            send_sem=v_send.at[way, block],
-            recv_sem=v_recv.at[block],
+            src_ref=vc.at[block, part],
+            dst_ref=vc.at[block, part],
+            send_sem=v_send.at[way, block, u],
+            recv_sem=v_recv.at[block, u],
             device_id=(to, my_q),
             device_id_type=MESH,
         )
@@ -92,21 +100,66 @@
             device_id_type=MESH,
         )
 
-    def pass_on(a):
-        block = 2 * a + x
-
-        @pl.when((a <= z) & (z < Z - 1))
-        def _():
-            v_copy(block, 0, up).start()
-
-        @pl.when((a >= z) & (z > 0))
-        def _():
-            v_copy(block, 1, down).start()
-
-        v_copy(block, 2, side).start()
-
-    pass_on(z)
-
+    def stream(way, s):
+        if way == 0:
+            return z - s, (z >= s) & (z < Z - 1), up
+        if way == 1:
+            return z + s, (z + s < Z) & (z > 0), down
+        return nth_nearest(s, z, Z), None, side
+
+    def each(way, n, act):
+        a, there, to = stream(way, n // CHUNKS)
+        copy = v_copy(2 * a + x, n % CHUNKS, way, to)
+        if there is None:
+            act(copy)
+        else:
+            pl.when(there)(lambda: act(copy))
+
+    def start(copy):
+        copy.start()
+
+    def wait_send(copy):
+        copy.wait_send()
+
+    def drain(way, n):
+        there = stream(way, n // CHUNKS)[1]
+        if there is None:
+            if n + WINDOW >= Z * CHUNKS:
+                each(way, n, wait_send)
+        elif n + WINDOW >= Z * CHUNKS:
+            each(way, n, wait_send)
+        else:
+            later = stream(way, (n + WINDOW) // CHUNKS)[1]
+
+            @pl.when(jnp.logical_not(later))
+            def _():
+                each(way, n, wait_send)
+
+    def tick(n):
+        s, u = n // CHUNKS, n % CHUNKS
+        if s > 0:
+
+            @pl.when(z >= s)
+            def _():
+                v_copy(2 * (z - s) + x, u, 0, side).wait_recv()
+
+            @pl.when(z + s < Z)
+            def _():
+                v_copy(2 * (z + s) + x, u, 0, side).wait_recv()
+
+        for way in range(3):
+            if n >= WINDOW:
+                a, there, to = stream(way, s)
+                if there is None:
+                    each(way, n - WINDOW, wait_send)
+                else:
+                    pl.when(there)(lambda: each(way, n - WINDOW, wait_send))
+            each(way, n, start)
+
+    for n in range(WINDOW):
+        tick(n)
+
+    load_tm.wait()
     load_t.wait()
     cd = tm_ref.shape[0]
     for i in range(tm_ref.shape[1]):
@@ -150,47 +203,40 @@
             else:
                 out_ref[:, cols] = part.astype(out_ref.dtype)
 
-    def take(s):
-        a = nth_nearest(s, z, Z)
-        v_copy(2 * a + x, 2, side).wait_recv()
-        pass_on(a)
-
     def finish(s):
         a = nth_nearest(s, z, Z)
-        v_copy(2 * a + (1 - x), 2, side).wait_recv()
+        for u in range(CHUNKS):
+            v_copy(2 * a + (1 - x), u, 2, side).wait_recv()
         multiply(a, s)
 
-    first = min(2, Z - 1)
-    for s in range(1, first + 1):
-        take(s)
-    for i in range(1, H):
-        block = 2 * lax.rem(h + H - i, H) + c
-        t_copy(block, t_far.at[i], sibling).wait_recv()
-        t_copy(block, t_near.at[block], sibling).start()
-    for i in range(H):
-        block = 2 * i + (1 - c)
-        t_copy(block, t_near.at[block], sibling).wait_recv()
-    for s in range(Z):
-        if s > first:
-            take(s)
-        if s >= first:
-            finish(s - first)
-    for s in range(Z - first, Z):
+    def t_onward():
+        for i in range(1, H):
+            block = 2 * lax.rem(h + H - i, H) + c
+            t_copy(block, t_far.at[i], sibling).wait_recv()
+            t_copy(block, t_near.at[block], sibling).start()
+
+    def t_arrived():
+        for i in range(H):
+            block = 2 * i + (1 - c)
+            t_copy(block, t_near.at[block], sibling).wait_recv()
+
+    done = 0
+    last = (Z - 1) * CHUNKS
+    for n in range(WINDOW, Z * CHUNKS):
+        tick(n)
+        if n == last:
+            t_onward()
+        if n == last + 1:
+            t_arrived()
+        if n >= last + 1 and done < Z - 1:
+            finish(done)
+            done += 1
+    for s in range(done, Z):
         finish(s)
 
-    for s in range(Z):
-        a = nth_nearest(s, z, Z)
-        block = 2 * a + x
-
-        @pl.when((a <= z) & (z < Z - 1))
-        def _():
-            v_copy(block, 0, up).wait_send()
-
-        @pl.when((a >= z) & (z > 0))
-        def _():
-            v_copy(block, 1, down).wait_send()
-
-        v_copy(block, 2, side).wait_send()
+    for n in range(Z * CHUNKS):
+        for way in range(3):
+            drain(way, n)
     for i in range(1, H):
         t_copy(my_q, t_far.at[i], sibling).wait_send()
     for i in range(H):
@@ -206,11 +252,12 @@
     bf16 = jnp.bfloat16
     return pl.pallas_call(
         functools.partial(kernel, n_pair // 2, n_virt // 2),
-        out_shape=jax.ShapeDtypeStruct((rows, ab_rows), bf16),
-        in_specs=[pl.BlockSpec(memory_space=pltpu.SMEM)] * 2
-        + [pl.BlockSpec(memory_space=pl.ANY)] * 2,
+        out_shape=pltpu.VMEM((rows, ab_rows), bf16),
+        in_specs=[pl.BlockSpec(memory_space=pl.ANY)] * 4,
         out_specs=pl.BlockSpec(memory_space=pltpu.VMEM),
         scratch_shapes=[
+            pltpu.SMEM(t_mask.shape[::-1], jnp.int32),
+            pltpu.SMEM(v_mask.shape, jnp.int32),
             pltpu.VMEM((rows, t_cols), bf16),
             pltpu.VMEM((ab_tiles, TILE, TILE), bf16),
             pltpu.VMEM((n_virt, rows, t_cols), bf16),
@@ -218,15 +265,15 @@
             pltpu.VMEM((VCAP + 1, TILE, TILE), bf16),
             pltpu.VMEM((ab_rows, 2 * TILE), bf16),
             pltpu.VMEM((rows, ab_rows), jnp.float32),
-            dma((2,)),
-            dma((n_pair,)),
-            dma((3, n_pair)),
+            dma((4,)),
+            dma((n_pair, CHUNKS)),
+            dma((3, n_pair, CHUNKS)),
             dma((n_virt,)),
             dma((n_virt,)),
             dma((n_virt,)),
         ],
         compiler_params=pltpu.CompilerParams(
-            collective_id=0, has_side_effects=True, vmem_limit_bytes=40 * 2**20
+            collective_id=0, has_side_effects=True, vmem_limit_bytes=60 * 2**20
         ),
     )(t_mask.T, v_mask, t_amps, v_ints.reshape(ab_tiles, TILE, TILE))
 

time: 29.9 us -> 22.4 us (0.75)
  Pallas kernels: 25.5 us -> 21 us
  local copies, waits for them, and re-layouts: 4.24 us -> 0.97 us
    pallas_call x1, Pallas kernels: 25.5 us -> 21 us  [local(): pl.pallas_call(functools.partial(kernel, n_pair // 2, n_virt // 2), out_s...]
    unnamed x9 -> x1, local copies, waits for them, and re-layouts: 4.24 us -> 0.97 us
where the time goes in v2:
time: 22.4 us; the launch traced here: 22 us
  Pallas kernels  21 us (94%)
  local copies, waits for them, and re-layouts  0.97 us (4%)
    pallas_call x1, Pallas kernels, local(): pl.pallas_call(functools.partial(kernel, n_pair // 2, n_virt // 2), out_s...  21 us
    unnamed x1, local copies, waits for them, and re-layouts  0.97 us

profile of v2, /device:TPU:0, one launch (start us, length us, event | category | flops | bytes accessed | tf_op | source)
XLA Modules:
  0.0 22.0 jit_solution(9693175053692774140)
XLA Ops:
  0.0 21.0 %shard_map.46 = bf16[512,1024]{1,0:T(8,128)(2,1)S(1)} custom-call(s32[2,4]{1,0:T(2,128)} %bitcast.3, s32[8,8]{1,0:T(8,128)} %vm_hbm.1, bf16[512,256]{1,0:T(8,128)(2,1)} %t_hbm.1, bf16[8,128,128]{2,1,0:T(8,128)(2,1)} %bitcast.2), custom_call_target="tpu_custom_call" | custom-call | tf_op jit(solution)/shard_map/pallas_call | solution.py:253
  21.0 1.0 %copy.6 = bf16[512,1024]{1,0:T(8,128)(2,1)} copy(bf16[512,1024]{1,0:T(8,128)(2,1)S(1)} %shard_map.46) | data formatting | bytes 2097152

commit v3 on v2

--- a/solution.py
+++ b/solution.py
@@ -224,11 +224,11 @@
     last = (Z - 1) * CHUNKS
     for n in range(WINDOW, Z * CHUNKS):
         tick(n)
-        if n == last:
+        if n == last - 1:
             t_onward()
-        if n == last + 1:
+        if n == last - 0:
             t_arrived()
-        if n >= last + 1 and done < Z - 1:
+        if n >= last - 0 and done < Z - 1:
             finish(done)
             done += 1
     for s in range(done, Z):

time: 22.4 us -> 23.4 us (1.045)
  Pallas kernels: 21 us -> 22.2 us
    pallas_call x1, Pallas kernels: 21 us -> 22.2 us  [local(): pl.pallas_call(functools.partial(kernel, n_pair // 2, n_virt // 2), out_s...]
where the time goes in v3:
time: 23.4 us; the launch traced here: 23.2 us
  Pallas kernels  22.2 us (95%)
  local copies, waits for them, and re-layouts  0.97 us (4%)
    pallas_call x1, Pallas kernels, local(): pl.pallas_call(functools.partial(kernel, n_pair // 2, n_virt // 2), out_s...  22.2 us
    unnamed x1, local copies, waits for them, and re-layouts  0.97 us

profile of v3, /device:TPU:0, one launch (start us, length us, event | category | flops | bytes accessed | tf_op | source)
XLA Modules:
  0.0 23.2 jit_solution(8160191707130801191)
XLA Ops:
  0.0 22.2 %shard_map.46 = bf16[512,1024]{1,0:T(8,128)(2,1)S(1)} custom-call(s32[2,4]{1,0:T(2,128)} %bitcast.3, s32[8,8]{1,0:T(8,128)} %vm_hbm.1, bf16[512,256]{1,0:T(8,128)(2,1)} %t_hbm.1, bf16[8,128,128]{2,1,0:T(8,128)(2,1)} %bitcast.2), custom_call_target="tpu_custom_call" | custom-call | tf_op jit(solution)/shard_map/pallas_call | solution.py:253
  22.2 1.0 %copy.6 = bf16[512,1024]{1,0:T(8,128)(2,1)} copy(bf16[512,1024]{1,0:T(8,128)(2,1)S(1)} %shard_map.46) | data formatting | bytes 2097152
